TPU v7x, 128 devices: a whole 4x4x4 slice. The times are simulated.
128 devices in a mesh: dp: 16 (over x_hi, z, core), tensor: 8 (over x_lo, y).
Axes of the slice: x: 4 (x_hi: 2, x_lo: 2; x = x_hi * 2 + x_lo), y: 4, z: 4, core: 2. Of those that a mesh axis runs over, the one named last changes fastest.
Arguments:
- grad_blocks: bfloat16 [256, 512, 512], P(None, ('dp', 'tensor')), may hold values from -1.1953125 to 1.1953125
- block_of_slot: int32 [256], replicated, may hold values from 0 to 255, each once
- left_basis: float32 [256, 512, 512], P(('dp', 'tensor'))
- right_basis: float32 [256, 512, 512], P(('dp', 'tensor'))
- left_gram: float32 [256, 512, 512], P(('dp', 'tensor')), as said below
- right_gram: float32 [256, 512, 512], P(('dp', 'tensor')), as said below
- moment_first: float32 [256, 512, 512], P(('dp', 'tensor')), may hold values from -1.8 to 1.8
- moment_second: float32 [256, 512, 512], P(('dp', 'tensor')), may hold values from 0.01 to 0.2
Outputs:
- update: float32 [256, 512, 512], P(None, ('dp', 'tensor'))
- new_left_gram: float32 [256, 512, 512], P(('dp', 'tensor'))
- new_right_gram: float32 [256, 512, 512], P(('dp', 'tensor'))
- new_first: float32 [256, 512, 512], P(('dp', 'tensor'))
- new_second: float32 [256, 512, 512], P(('dp', 'tensor'))
Inputs may be any that keep to these rules, and one draw needn't show every extreme that they name: `block_of_slot`: each block appears in exactly one slot; slot s belongs to the device of flat index s // 2 over dp then tensor. `left_gram`: symmetric. `right_gram`: symmetric.
All inputs are finite; a program needn't handle non-finite values.
Results may differ from a plain program's by a relative error of at most 0.0003.
Values may be sent and summed in bfloat16 or wider, within the bound.
A program may use at most 128 MiB of HBM per device.

v0:
```python
import jax
import jax.numpy as jnp
from jax import lax
from jax.sharding import PartitionSpec as P


def local(
    grad_blocks,
    block_of_slot,
    left_basis,
    right_basis,
    left_gram,
    right_gram,
    moment_first,
    moment_second,
):
    hi = lax.Precision.HIGHEST
    n_data = lax.axis_size("dp")
    n_model = lax.axis_size("tensor")
    owned_count = left_basis.shape[0]
    rows = grad_blocks.shape[1]
    order = grad_blocks.shape[2]
    slotted = jnp.take(grad_blocks, block_of_slot, axis=0)
    arranged = slotted.reshape(n_data * n_model, owned_count, rows, order)
    arrived = lax.all_to_all(arranged, ("dp", "tensor"), split_axis=0, concat_axis=2, tiled=True)
    owned = arrived.reshape(owned_count, order, order).astype(jnp.float32)
    left_t = jnp.swapaxes(left_basis, 1, 2)
    right_t = jnp.swapaxes(right_basis, 1, 2)
    rotated = jnp.matmul(jnp.matmul(left_t, owned, precision=hi), right_basis, precision=hi)
    new_first = 0.9 * moment_first + 0.1 * rotated
    new_second = 0.95 * moment_second + 0.05 * rotated * rotated
    normalized = new_first / (jnp.sqrt(new_second) + 1e-08)
    result = jnp.matmul(jnp.matmul(left_basis, normalized, precision=hi), right_t, precision=hi)
    owned_t = jnp.swapaxes(owned, 1, 2)
    new_lgram = 0.95 * left_gram + 0.05 * jnp.matmul(owned, owned_t, precision=hi)
    new_rgram = 0.95 * right_gram + 0.05 * jnp.matmul(owned_t, owned, precision=hi)
    outgoing = result.reshape(1, owned_count, n_data * n_model, rows, order)
    returned = lax.all_to_all(outgoing, ("dp", "tensor"), split_axis=2, concat_axis=0, tiled=True)
    returned = returned.reshape(block_of_slot.shape[0], rows, order)
    update = jnp.zeros(returned.shape, jnp.float32).at[block_of_slot].set(returned)
    return (update, new_lgram, new_rgram, new_first, new_second)


def solution(mesh):
    return jax.shard_map(
        local,
        mesh=mesh,
        in_specs=(
            P(None, ("dp", "tensor"), None),
            P(),
            P(("dp", "tensor"), None, None),
            P(("dp", "tensor"), None, None),
            P(("dp", "tensor"), None, None),
            P(("dp", "tensor"), None, None),
            P(("dp", "tensor"), None, None),
            P(("dp", "tensor"), None, None),
        ),
        out_specs=(
            P(None, ("dp", "tensor"), None),
            P(("dp", "tensor"), None, None),
            P(("dp", "tensor"), None, None),
            P(("dp", "tensor"), None, None),
            P(("dp", "tensor"), None, None),
        ),
        check_vma=False,
    )
```

profile of v0, /device:TPU:1, one launch (start us, length us, event | category | flops | bytes accessed | tf_op | source)
XLA Modules:
  0.0 129.6 jit_solution(501178228765693080)
XLA Ops:
  0.6 0.0 copy-start
  0.6 0.8 compare_select_fusion
  1.5 0.7 compare_and_fusion
  2.2 0.2 broadcast_in_dim.20
  2.3 2.8 %gather_fusion = bf16[256,4,512]{2,1,0:T(4,128)(2,1)S(1)} fusion(bf16[256,4,512]{2,1,0:T(4,128)(2,1)} %param.8, s32[1024]{0:T(1024)S(1)} %pad_clamp_fusion), kind=kCustom, calls=%fused_computation | custom fusion | bytes 2098176 | tf_op jit(solution)/shard_map/jit(_take)/gather | solution.py:23
  5.1 0.7 broadcast_select_fusion
  5.8 30.1 %all_to_all.30 = bf16[128,2,4,512]{3,2,1,0:T(4,128)(2,1)S(1)} all-to-all(bf16[128,2,4,512]{3,2,1,0:T(4,128)(2,1)S(1)} %broadcast_select_fusion), channel_id=1, replica_groups=mesh['dp'=16,'tensor'=8] {'dp','tensor'}, dimensions={0} | all-to-all | bytes 2097152 | tf_op jit(solution)/shard_map/all_to_all | solution.py:25
  35.9 0.8 copy.28
  36.8 2.5 %copy.29 = bf16[2,512,512]{1,2,0:T(8,128)(2,1)} copy(bf16[2,512,512]{2,0,1:T(2,128)(2,1)S(1)} %bitcast.18) | data formatting | bytes 2097152 | tf_op jit(solution)/shard_map/reshape | solution.py:26
  39.3 0.0 copy-start.4
  39.3 0.0 copy-start.5
  39.3 3.9 %fusion.9 = f32[2,512,512]{1,2,0:T(8,128)S(1)} fusion(bf16[2,512,512]{1,2,0:T(8,128)(2,1)} %copy.29, f32[2,512,512]{2,1,0:T(8,128)} %param.10), kind=kOutput, calls=%fused_computation.19 | convolution fusion | flops 3221225472 | bytes 5242880 | tf_op jit(solution)/shard_map/dot_general | solution.py:29
  43.2 0.0 copy-done
  43.2 0.0 copy-done.4
  43.2 0.0 copy-done.5
  43.2 0.0 copy-start.3
  43.2 3.8 %fusion = (f32[2,512,512]{2,1,0:T(8,128)S(1)}, f32[2,512,512]{2,1,0:T(8,128)S(1)}) fusion(f32[2,512,512]{2,1,0:T(8,128)S(1)} %copy-done.4, f32[2,512,512]{2,1,0:T(8,128)S(1)} %copy-done.5, f32[2,512,512]{1,2,0:T(8,128)S(1)} %fusion.9, f32[2,512,512]{2,1,0:T(8,128)S(1)} %copy-done), kind=kOutput, calls=%fused_computation.3 | convolution fusion | flops 3224895488 | bytes 12582912 | tf_op jit(solution)/shard_map/dot_general | solution.py:29
  47.1 0.0 copy-start.6
  47.1 0.0 copy-start.7
  47.1 0.0 copy-done.3
  47.1 4.2 %fusion.1 = f32[2,512,512]{1,2,0:T(8,128)S(1)} fusion(f32[2,512,512]{2,1,0:T(8,128)S(1)} %copy-done.3, f32[2,512,512]{2,1,0:T(8,128)S(1)} %get-tuple-element.6, f32[2,512,512]{2,1,0:T(8,128)S(1)} %get-tuple-element.5), kind=kOutput, calls=%fused_computation.6 | convolution fusion | flops 3222274048 | bytes 8388608 | tf_op jit(solution)/shard_map/dot_general | solution.py:33
  51.3 0.0 copy-done.6
  51.3 0.0 copy-done.7
  51.3 5.1 %fusion.10 = f32[2,512,512]{2,1,0:T(8,128)} fusion(f32[2,512,512]{1,2,0:T(8,128)S(1)} %fusion.1, f32[2,512,512]{2,1,0:T(8,128)S(1)} %copy-done), kind=kOutput, calls=%fused_computation.20 | convolution fusion | flops 3221225472 | bytes 6291456 | tf_op jit(solution)/shard_map/dot_general | solution.py:33
  56.4 2.8 %reshape.31 = f32[1,2,128,4,512]{4,3,2,1,0:T(4,128)} reshape(f32[2,512,512]{2,1,0:T(8,128)} %fusion.10) | data formatting | bytes 4194304 | tf_op jit(solution)/shard_map/reshape | solution.py:37
  59.3 3.6 %copy.33 = f32[1,2,128,4,512]{4,3,1,0,2:T(4,128)} copy(f32[1,2,128,4,512]{4,3,2,1,0:T(4,128)} %reshape.31) | data formatting | bytes 4194304 | tf_op jit(solution)/shard_map/reshape | solution.py:37
  62.9 5.8 %all-to-all-start.1 = ((f32[1,2,128,4,512]{4,3,1,0,2:T(4,128)}), f32[1,2,128,4,512]{4,3,1,0,2:T(4,128)}, u32[]{:S(2)}, u32[]{:S(2)}) async-start(f32[1,2,128,4,512]{4,3,1,0,2:T(4,128)} %copy.33), calls=%async_computation.1 | async-start | bytes 4194304 | tf_op jit(solution)/shard_map/all_to_all | solution.py:38
  68.7 0.0 copy-start.1
  68.7 0.0 copy-start.2
  68.7 3.9 %multiply_add_fusion.1 = f32[2,512,512]{2,1,0:T(8,128)} fusion(f32[2,512,512]{2,1,0:T(8,128)} %param.12, bf16[2,512,512]{2,0,1:T(2,128)(2,1)S(1)} %bitcast.19), kind=kOutput, calls=%fused_computation.5 | convolution fusion | flops 538443776 | bytes 5242880 | tf_op jit(solution)/shard_map/dot_general | solution.py:35
  72.6 0.0 copy-done.1
  72.6 0.0 copy-done.2
  72.6 2.1 %multiply_add_fusion = f32[2,512,512]{2,1,0:T(8,128)} fusion(f32[2,512,512]{2,1,0:T(8,128)S(1)} %copy-done.2, bf16[2,512,512]{1,2,0:T(8,128)(2,1)S(1)} %copy-done.1, bf16[2,512,512]{2,0,1:T(2,128)(2,1)S(1)} %bitcast.20), kind=kOutput, calls=%fused_computation.4 | convolution fusion | flops 538443776 | bytes 6291456 | tf_op jit(solution)/shard_map/dot_general | solution.py:36
  74.7 23.3 %all-to-all-done.1 = f32[1,2,128,4,512]{4,3,1,0,2:T(4,128)} async-done(((f32[1,2,128,4,512]{4,3,1,0,2:T(4,128)}), f32[1,2,128,4,512]{4,3,1,0,2:T(4,128)}, u32[]{:S(2)}, u32[]{:S(2)}) %all-to-all-start.1) | async-done | bytes 2097184 | tf_op jit(solution)/shard_map/all_to_all | solution.py:38
  98.1 1.6 %broadcast_in_dim.18 = f32[256,4,512]{2,1,0:T(4,128)} broadcast(f32[]{:T(128)} %constant.10.clone.1), dimensions={} | broadcast | bytes 2097156 | tf_op jit(solution)/shard_map/broadcast_in_dim | solution.py:40
  99.7 29.9 %scatter_fusion = f32[256,4,512]{2,1,0:T(4,128)} fusion(f32[256,4,512]{2,1,0:T(4,128)} %broadcast_in_dim.18, s32[256]{0:T(256)S(1)} %compare_select_fusion, f32[256,4,512]{2,1,0:T(4,128)} %bitcast.6), kind=kCustom, calls=%fused_computation.1 | custom fusion | bytes 6292480 | tf_op jit(solution)/shard_map/scatter | solution.py:40
  (1 shorter events, 0.0 us)
Async XLA Ops:
  0.6 42.5 %copy-start = (f32[2,512,512]{2,1,0:T(8,128)S(1)}, f32[2,512,512]{2,1,0:T(8,128)}, u32[]{:S(2)}) copy-start(f32[2,512,512]{2,1,0:T(8,128)} %param.11) | copy-start | bytes 6291460
  39.3 3.9 %copy-start.4 = (f32[2,512,512]{2,1,0:T(8,128)S(1)}, f32[2,512,512]{2,1,0:T(8,128)}, u32[]{:S(2)}) copy-start(f32[2,512,512]{2,1,0:T(8,128)} %param.15) | copy-start | bytes 6291460
  39.3 3.9 %copy-start.5 = (f32[2,512,512]{2,1,0:T(8,128)S(1)}, f32[2,512,512]{2,1,0:T(8,128)}, u32[]{:S(2)}) copy-start(f32[2,512,512]{2,1,0:T(8,128)} %param.14) | copy-start | bytes 6291460
  43.2 3.9 %copy-start.3 = (f32[2,512,512]{2,1,0:T(8,128)S(1)}, f32[2,512,512]{2,1,0:T(8,128)}, u32[]{:S(2)}) copy-start(f32[2,512,512]{2,1,0:T(8,128)} %param.10) | copy-start | bytes 6291460
  47.1 4.2 %copy-start.6 = (f32[2,512,512]{2,1,0:T(8,128)}, f32[2,512,512]{2,1,0:T(8,128)S(1)}, u32[]{:S(2)}) copy-start(f32[2,512,512]{2,1,0:T(8,128)S(1)} %get-tuple-element.5) | copy-start | bytes 6291460
  47.1 4.2 %copy-start.7 = (f32[2,512,512]{2,1,0:T(8,128)}, f32[2,512,512]{2,1,0:T(8,128)S(1)}, u32[]{:S(2)}) copy-start(f32[2,512,512]{2,1,0:T(8,128)S(1)} %get-tuple-element.6) | copy-start | bytes 6291460
  62.9 35.2 %all-to-all-start.1 = ((f32[1,2,128,4,512]{4,3,1,0,2:T(4,128)}), f32[1,2,128,4,512]{4,3,1,0,2:T(4,128)}, u32[]{:S(2)}, u32[]{:S(2)}) async-start(f32[1,2,128,4,512]{4,3,1,0,2:T(4,128)} %copy.33), calls=%async_computation.1 | async-start | bytes 4194304 | tf_op jit(solution)/shard_map/all_to_all | solution.py:38
  68.7 4.0 %copy-start.1 = (bf16[2,512,512]{1,2,0:T(8,128)(2,1)S(1)}, bf16[2,512,512]{1,2,0:T(8,128)(2,1)}, u32[]{:S(2)}) copy-start(bf16[2,512,512]{1,2,0:T(8,128)(2,1)} %copy.29) | copy-start | bytes 3145732
  68.7 3.9 %copy-start.2 = (f32[2,512,512]{2,1,0:T(8,128)S(1)}, f32[2,512,512]{2,1,0:T(8,128)}, u32[]{:S(2)}) copy-start(f32[2,512,512]{2,1,0:T(8,128)} %param.13) | copy-start | bytes 6291460
where the time goes:
time: 130 us
  local copies, waits for them, and re-layouts  44.3 us (34%)
  blocking collectives  30.1 us (23%)
  waiting for transfers between devices  23.3 us (18%)
  matrix products  23 us (18%)
  starting transfers between devices  5.77 us (4%)
  other arithmetic  2.25 us (2%)
    all_to_all x1, blocking collectives, local(): lax.all_to_all(arranged, ('dp', 'tensor'), split_axis=0, concat_axis=2, t...  30.1 us
    scatter x1, local copies, waits for them, and re-layouts, local(): jnp.zeros(returned.shape, jnp.float32).at[block_of_slot].set(returned)  29.9 us
    all_to_all x1, waiting for transfers between devices, local(): lax.all_to_all(outgoing, ('dp', 'tensor'), split_axis=2, concat_axis=0, t...  23.3 us
    reshape x2, local copies, waits for them, and re-layouts, local(): outgoing = result.reshape(1, owned_count, n_data * n_model, rows, order)  6.49 us
    all_to_all x1, starting transfers between devices, local(): lax.all_to_all(outgoing, ('dp', 'tensor'), split_axis=2, concat_axis=0, t...  5.77 us
    dot_general x1, matrix products, local(): jnp.matmul(jnp.matmul(left_basis, normalized, precision=hi), right_t, pre...  5.09 us
    dot_general x1, matrix products, local(): jnp.matmul(left_basis, normalized, precision=hi)  4.19 us
    dot_general x1, matrix products, local(): jnp.matmul(owned, owned_t, precision=hi)  3.93 us
  transfers between devices with their start and end apart: 1, of which 1 were waited for; matrix products, arithmetic and copies ran while one was open for 5% of the time, Pallas kernels for 0%

commit v1 on v0

v1 whole, which is shorter than its diff:
```python
import jax
import jax.numpy as jnp
from jax import lax
from jax.experimental import pallas as pl
from jax.experimental.pallas import tpu as pltpu
from jax.sharding import PartitionSpec as P

MESH = pl.DeviceIdType.MESH
F32 = jnp.float32
BF16 = jnp.bfloat16
N = 512
DP, TP = 16, 8
DEV = DP * TP
CH = 128
GROUP = CH // 4
LEVELS = 32767.0


def split(x):
    hi = x.astype(BF16)
    return hi, (x - hi.astype(F32)).astype(BF16)


def dot(a, b):
    return jnp.dot(a, b, preferred_element_type=F32)


def dot_nt(a, b):
    return lax.dot_general(a, b, (((1,), (1,)), ((), ())), preferred_element_type=F32)


def dot_tn(a, b):
    return lax.dot_general(a, b, (((0,), (0,)), ((), ())), preferred_element_type=F32)


def exchange_kernel(
    bos,
    grad,
    left_h,
    right_h,
    lgram_h,
    rgram_h,
    first_h,
    second_h,
    codes,
    scales,
    nlgram,
    nrgram,
    nfirst,
    nsecond,
    left,
    right,
    lgram,
    rgram,
    first,
    second,
    lt_hi,
    lt_lo,
    l_hi,
    l_lo,
    r_hi,
    r_lo,
    stage_in,
    land_in,
    owned,
    n_hi,
    n_lo,
    stage_out,
    stage_scale,
    load_sem,
    in_send,
    in_recv,
    out_send,
    out_recv,
    sc_sem,
):
    dp = lax.axis_index("dp")
    tp = lax.axis_index("tensor")
    me = dp * TP + tp

    loads = [
        pltpu.make_async_copy(src, dst, load_sem.at[i])
        for i, (src, dst) in enumerate(
            ((left_h, left), (right_h, right), (first_h, first), (second_h, second), (lgram_h, lgram), (rgram_h, rgram))
        )
    ]
    for load in loads:
        load.start()

    barrier = pltpu.get_barrier_semaphore()

    def greet(d, t):
        pl.semaphore_signal(barrier, inc=1, device_id=(d, t), device_id_type=MESH)

    for i in range(1, TP):
        greet(dp, (tp + i) & (TP - 1))

    @pl.loop(1, DP)
    def _(j):
        for i in range(TP):
            greet((dp + j) & (DP - 1), (tp + i) & (TP - 1))

    for s in range(2):

        @pl.loop(0, DEV, step=8)
        def _(p):
            for i in range(8):
                stage_in[s, p + i] = grad[bos[2 * (p + i) + s]]

        land_in[s, me] = stage_in[s, me]

    pl.semaphore_wait(barrier, DEV - 1)

    def send_in(s, d, t):
        pltpu.make_async_remote_copy(
            stage_in.at[s, d * TP + t],
            land_in.at[s, me],
            in_send.at[s],
            in_recv.at[s],
            device_id=(d, t),
            device_id_type=MESH,
        ).start()

    for s in range(2):
        for i in range(1, TP):
            send_in(s, dp, (tp + i) & (TP - 1))

        @pl.loop(1, DP)
        def _(j):
            for i in range(TP):
                send_in(s, (dp + j) & (DP - 1), (tp + i) & (TP - 1))

    loads[0].wait()
    loads[1].wait()
    for s in range(2):

        @pl.loop(0, N, step=CH)
        def _(r):
            rows = pl.ds(pl.multiple_of(r, CH), CH)
            hi, lo = split(left[s, rows, :])
            l_hi[s, rows, :] = hi
            l_lo[s, rows, :] = lo
            hi, lo = split(right[s, rows, :])
            r_hi[s, rows, :] = hi
            r_lo[s, rows, :] = lo
            hi, lo = split(left[s, :, rows].T)
            lt_hi[s, rows, :] = hi
            lt_lo[s, rows, :] = lo

    loads[2].wait()
    loads[3].wait()

    def all_of(ref, sem):
        pltpu.make_async_copy(ref, ref, sem).wait()

    for s in range(2):
        all_of(land_in.at[s, pl.ds(0, DEV - 1)], in_recv.at[s])
        for c in range(4):
            owned[s, :, c * 128 : (c + 1) * 128] = land_in[s, :, 4 * c : 4 * c + 4, :].reshape(N, 128)

        @pl.loop(0, N, step=CH)
        def _(r):
            rows = pl.ds(pl.multiple_of(r, CH), CH)
            block = owned[s]
            a = dot(lt_hi[s, rows, :], block) + dot(lt_lo[s, rows, :], block)
            a_hi, a_lo = split(a)
            rotated = dot(a_hi, r_hi[s]) + (dot(a_hi, r_lo[s]) + dot(a_lo, r_hi[s]))
            nf = 0.9 * first[s, rows, :] + 0.1 * rotated
            ns = 0.95 * second[s, rows, :] + 0.05 * rotated * rotated
            nfirst[s, rows, :] = nf
            nsecond[s, rows, :] = ns
            hi, lo = split(nf / (jnp.sqrt(ns) + 1e-08))
            n_hi[rows, :] = hi
            n_lo[rows, :] = lo

        @pl.loop(0, N // CH)
        def _(j):
            chunk = (dp // (GROUP // TP) + j) & (N // CH - 1)
            rows = pl.ds(pl.multiple_of(chunk * CH, CH), CH)
            b = dot(l_hi[s, rows, :], n_hi[...]) + (dot(l_hi[s, rows, :], n_lo[...]) + dot(l_lo[s, rows, :], n_hi[...]))
            b_hi, b_lo = split(b)
            result = dot_nt(b_hi, r_hi[s]) + (dot_nt(b_hi, r_lo[s]) + dot_nt(b_lo, r_hi[s]))
            top = jnp.maximum(jnp.max(jnp.abs(result), axis=1, keepdims=True), 1e-33)
            q = jnp.clip(jnp.round(result * (LEVELS / top)), -LEVELS, LEVELS).astype(jnp.int32)
            packed = (q[:, : N // 2] & 0xFFFF) | (q[:, N // 2 :] << 16)
            first_dev = pl.multiple_of(chunk * GROUP, GROUP)
            for c in range(2):
                stage_out[s, pl.ds(first_dev, GROUP), 4 * c : 4 * c + 4, :] = packed[
                    :, c * 128 : (c + 1) * 128
                ].reshape(GROUP, 4, 128)
            step = jnp.broadcast_to(top * (1.0 / LEVELS), (CH, 128)).T
            stage_scale[chunk, s] = step[:1, :]

            @pl.loop(0, GROUP // TP)
            def _(g):
                d = chunk * (GROUP // TP) + ((dp + g) & (GROUP // TP - 1))
                for i in range(TP):
                    t = (tp + i) & (TP - 1)

                    def send_out():
                        pltpu.make_async_remote_copy(
                            stage_out.at[s, d * TP + t],
                            codes.at[s, me],
                            out_send.at[s],
                            out_recv.at[s],
                            device_id=(d, t),
                            device_id_type=MESH,
                        ).start()
                        if s == 1:
                            pltpu.make_async_remote_copy(
                                stage_scale.at[chunk],
                                scales.at[me],
                                sc_sem.at[0],
                                sc_sem.at[1],
                                device_id=(d, t),
                                device_id_type=MESH,
                            ).start()

                    if i:
                        send_out()
                    else:
                        pl.when(d != dp)(send_out)

        codes[s, me] = stage_out[s, me]

    scales[me] = stage_scale[dp // (GROUP // TP)]

    loads[4].wait()
    loads[5].wait()
    for s in range(2):

        @pl.loop(0, N, step=CH)
        def _(r):
            rows = pl.ds(pl.multiple_of(r, CH), CH)
            nlgram[s, rows, :] = 0.95 * lgram[s, rows, :] + 0.05 * dot_nt(owned[s, rows, :], owned[s])
            nrgram[s, rows, :] = 0.95 * rgram[s, rows, :] + 0.05 * dot_tn(owned[s, :, rows], owned[s])

    for s in range(2):
        all_of(land_in.at[s, pl.ds(0, DEV - 1)], in_send.at[s])
        all_of(codes.at[s, pl.ds(0, DEV - 1)], out_send.at[s])
        all_of(codes.at[s, pl.ds(0, DEV - 1)], out_recv.at[s])
        all_of(scales.at[pl.ds(0, DEV - 1)], sc_sem.at[s])


def finish_kernel(bos, codes, scales, nlgram, nrgram, nfirst, nsecond, update, o_l, o_r, o_f, o_s, upd, sem):
    me = lax.axis_index("dp") * TP + lax.axis_index("tensor")
    moves = [
        pltpu.make_async_copy(src, dst, sem.at[i])
        for i, (src, dst) in enumerate(((nlgram, o_l), (nrgram, o_r), (nfirst, o_f), (nsecond, o_s)))
    ]
    for move in moves:
        move.start()
    lane = lax.broadcasted_iota(jnp.int32, (8, 128), 1)
    row = lax.broadcasted_iota(jnp.int32, (8, 128), 0)
    mine = lane == (me & (GROUP - 1)) * 4 + (row & 3)

    for s in range(2):

        @pl.loop(0, DEV, step=8)
        def _(p):
            for i in range(8):
                b = bos[2 * (p + i) + s]
                v = codes[s, p + i]
                step = jnp.sum(
                    jnp.where(mine, jnp.broadcast_to(scales[p + i, s], (8, 128)), 0.0), axis=1, keepdims=True
                )
                upd[b, 0:8, :] = ((v << 16) >> 16).astype(F32) * step
                upd[b, 8:16, :] = (v >> 16).astype(F32) * step

    out = pltpu.make_async_copy(upd, update, sem.at[4])
    out.start()
    for move in moves:
        move.wait()
    out.wait()


def local(grad_blocks, block_of_slot, left_basis, right_basis, left_gram, right_gram, moment_first, moment_second):
    blocks = grad_blocks.shape[0]
    grad = grad_blocks.reshape(blocks, 4, 4, 128).transpose(0, 2, 1, 3).reshape(blocks, 16, 128)
    hbm = pl.BlockSpec(memory_space=pltpu.HBM)
    vmem = pl.BlockSpec(memory_space=pltpu.VMEM)
    smem = pl.BlockSpec(memory_space=pltpu.SMEM)
    square = (2, N, N)
    codes, scales, nlgram, nrgram, nfirst, nsecond = pl.pallas_call(
        exchange_kernel,
        out_shape=(
            pltpu.VMEM((2, DEV, 8, 128), jnp.int32),
            pltpu.VMEM((DEV, 2, 1, 128), F32),
            pltpu.VMEM(square, F32),
            pltpu.VMEM(square, F32),
            pltpu.VMEM(square, F32),
            pltpu.VMEM(square, F32),
        ),
        in_specs=[smem, vmem] + [hbm] * 6,
        out_specs=(vmem,) * 6,
        scratch_shapes=[pltpu.VMEM(square, F32)] * 6
        + [pltpu.VMEM(square, BF16)] * 6
        + [
            pltpu.VMEM((2, DEV, 16, 128), BF16),
            pltpu.VMEM((2, DEV, 16, 128), BF16),
            pltpu.VMEM(square, BF16),
            pltpu.VMEM((N, N), BF16),
            pltpu.VMEM((N, N), BF16),
            pltpu.VMEM((2, DEV, 8, 128), jnp.int32),
            pltpu.VMEM((N // CH, 2, 1, 128), F32),
            pltpu.SemaphoreType.DMA((6,)),
            pltpu.SemaphoreType.DMA((2,)),
            pltpu.SemaphoreType.DMA((2,)),
            pltpu.SemaphoreType.DMA((2,)),
            pltpu.SemaphoreType.DMA((2,)),
            pltpu.SemaphoreType.DMA((2,)),
        ],
        compiler_params=pltpu.CompilerParams(collective_id=0, has_side_effects=True, vmem_limit_bytes=40 << 20),
        name="exchange",
    )(block_of_slot, grad, left_basis, right_basis, left_gram, right_gram, moment_first, moment_second)
    update, *rest = pl.pallas_call(
        finish_kernel,
        out_shape=(jax.ShapeDtypeStruct((blocks, 16, 128), F32),) + (jax.ShapeDtypeStruct(square, F32),) * 4,
        in_specs=[smem] + [vmem] * 6,
        out_specs=(hbm,) * 5,
        scratch_shapes=[pltpu.VMEM((blocks, 16, 128), F32), pltpu.SemaphoreType.DMA((5,))],
        compiler_params=pltpu.CompilerParams(vmem_limit_bytes=16 << 20),
        name="finish",
    )(block_of_slot, codes, scales, nlgram, nrgram, nfirst, nsecond)
    update = update.reshape(blocks, 4, 4, 128).transpose(0, 2, 1, 3).reshape(blocks, 4, N)
    return (update, *rest)


def solution(mesh):
    owner = P(("dp", "tensor"), None, None)
    rows = P(None, ("dp", "tensor"), None)
    return jax.shard_map(
        local,
        mesh=mesh,
        in_specs=(rows, P(), owner, owner, owner, owner, owner, owner),
        out_specs=(rows, owner, owner, owner, owner),
        check_vma=False,
    )
```

time: 130 us -> 56.5 us (0.43)
  Pallas kernels: 0 us -> 52.2 us
  local copies, waits for them, and re-layouts: 44.3 us -> 3.49 us
  blocking collectives: 30.1 us -> 0 us
  waiting for transfers between devices: 23.3 us -> 0 us
  matrix products: 23 us -> 0 us
  starting transfers between devices: 5.77 us -> 0 us
  other arithmetic: 2.25 us -> 0 us
    pallas_call x0 -> x2, Pallas kernels: none -> 52.2 us  [the longest x1 47.6 us: local(): pl.pallas_call(exchange_kernel, out_shape=(pltpu.VMEM((2, DEV, 8, 128), j...]
    all_to_all x1 -> x0, blocking collectives: 30.1 us -> none  [local(): lax.all_to_all(arranged, ('dp', 'tensor'), split_axis=0, concat_axis=2, t...]
    scatter x1 -> x0, local copies, waits for them, and re-layouts: 29.9 us -> none  [local(): jnp.zeros(returned.shape, jnp.float32).at[block_of_slot].set(returned)]
    all_to_all x1 -> x0, waiting for transfers between devices: 23.3 us -> none  [local(): lax.all_to_all(outgoing, ('dp', 'tensor'), split_axis=2, concat_axis=0, t...]
    dot_general x6 -> x0, matrix products: 23 us -> none  [the longest x1 5.09 us: local(): jnp.matmul(jnp.matmul(left_basis, normalized, precision=hi), right_t, pre...]
    reshape x3 -> x0, local copies, waits for them, and re-layouts: 8.98 us -> none  [the longest x2 6.49 us: local(): outgoing = result.reshape(1, owned_count, n_data * n_model, rows, order)]
    all_to_all x1 -> x0, starting transfers between devices: 5.77 us -> none  [local(): lax.all_to_all(outgoing, ('dp', 'tensor'), split_axis=2, concat_axis=0, t...]
    unnamed x16 -> x6, local copies, waits for them, and re-layouts: 0.05 us -> 3.49 us
  transfers between devices with their start and end apart: 1 -> 0, of which waited for: 1 -> 0; matrix products, arithmetic and copies ran while one was open for 5% -> 0% of each run, Pallas kernels for 0% -> 0%
where the time goes in v1:
time: 56.5 us; the launch traced here: 56.3 us
  Pallas kernels  52.2 us (92%)
  local copies, waits for them, and re-layouts  3.49 us (6%)
  between operations  0.65 us (1%)
    pallas_call x1, Pallas kernels, local(): pl.pallas_call(exchange_kernel, out_shape=(pltpu.VMEM((2, DEV, 8, 128), j...  47.6 us
    pallas_call x1, Pallas kernels, local(): pl.pallas_call(finish_kernel, out_shape=(jax.ShapeDtypeStruct((blocks, 16...  4.62 us
    unnamed x6, local copies, waits for them, and re-layouts  3.49 us

profile of v1, /device:TPU:1, one launch (start us, length us, event | category | flops | bytes accessed | tf_op | source)
XLA Modules:
  0.0 56.3 jit_solution(15329704814346905182)
XLA Ops:
  0.6 0.0 copy-start
  0.6 1.6 %copy-done = f32[2,512,512]{2,1,0:T(8,128)S(1)} copy-done((f32[2,512,512]{2,1,0:T(8,128)S(1)}, f32[2,512,512]{2,1,0:T(8,128)}, u32[]{:S(2)}) %copy-start) | copy-done | bytes 2097176
  2.2 0.0 copy-start.1
  2.2 1.2 %copy-done.1 = bf16[256,4,512]{2,1,0:T(4,128)(2,1)S(1)} copy-done((bf16[256,4,512]{2,1,0:T(4,128)(2,1)S(1)}, bf16[256,4,512]{2,1,0:T(4,128)(2,1)}, u32[]{:S(2)}) %copy-start.1) | copy-done | bytes 1048600
  3.5 0.0 copy-start.2
  3.5 0.7 %copy-done.2 = s32[256]{0:T(256)S(1)} copy-done((s32[256]{0:T(256)S(1)}, s32[256]{0:T(256)}, u32[]{:S(2)}) %copy-start.2) | copy-done | bytes 1048
  4.1 47.6 %exchange.1 = (s32[2,128,8,128]{3,2,1,0:T(8,128)S(1)}, f32[128,2,1,128]{3,2,1,0:T(1,128)S(1)}, f32[2,512,512]{2,1,0:T(8,128)S(1)}, f32[2,512,512]{2,1,0:T(8,128)...) custom-call(s32[256]{0:T(256)S(1)} %copy-done.2, bf16[256,16,128]{2,1,0:T(8,128)(2,1)S(1)} %bitcast.10, ...), custom_call_target="tpu_custom_call" | custom-call | tf_op jit(solution)/shard_map/exchange/pallas_call | solution.py:284
  51.7 4.6 %finish.1 = (f32[256,16,128]{2,1,0:T(8,128)}, f32[2,512,512]{2,1,0:T(8,128)}, f32[2,512,512]{2,1,0:T(8,128)}, f32[2,512,512]{2,1,0:T(8,128)}, f32[2,512,512]{2,1,0:T(8,128)}) custom-call(s32[256]{0:T(256)S(1)} %copy-done.2, s32[2,128,8,128]{3,2,1,0:T(8,128)S(1)} %get-tuple-element.16.codes, f32[128,2,1,128]{3,2,1,0:T(1,128)S(1)} %get-tuple-element.17.scales, ...), custom_call_target="tpu_custom_call" | custom-call | tf_op jit(solution)/shard_map/finish/pallas_call | solution.py:316
Async XLA Ops:
  0.6 1.6 %copy-start = (f32[2,512,512]{2,1,0:T(8,128)S(1)}, f32[2,512,512]{2,1,0:T(8,128)}, u32[]{:S(2)}) copy-start(f32[2,512,512]{2,1,0:T(8,128)} %left_h.1) | copy-start | bytes 6291460
  2.2 1.2 %copy-start.1 = (bf16[256,4,512]{2,1,0:T(4,128)(2,1)S(1)}, bf16[256,4,512]{2,1,0:T(4,128)(2,1)}, u32[]{:S(2)}) copy-start(bf16[256,4,512]{2,1,0:T(4,128)(2,1)} %param.8) | copy-start | bytes 3145732
  3.5 0.7 %copy-start.2 = (s32[256]{0:T(256)S(1)}, s32[256]{0:T(256)}, u32[]{:S(2)}) copy-start(s32[256]{0:T(256)} %bos.3) | copy-start | bytes 3076

commit v2 on v1

v2 whole, which is shorter than its diff:
```python
import jax
import jax.numpy as jnp
from jax import lax
from jax.experimental import pallas as pl
from jax.experimental.pallas import tpu as pltpu
from jax.sharding import PartitionSpec as P

MESH = pl.DeviceIdType.MESH
F32 = jnp.float32
BF16 = jnp.bfloat16
N = 512
DP, TP = 16, 8
DEV = DP * TP
LEVELS = 32767.0


def split(x):
    hi = x.astype(BF16)
    return hi, (x - hi.astype(F32)).astype(BF16)


def dot(a, b):
    return jnp.dot(a, b, preferred_element_type=F32)


def dot_nt(a, b):
    return lax.dot_general(a, b, (((1,), (1,)), ((), ())), preferred_element_type=F32)


def dot_tn(a, b):
    return lax.dot_general(a, b, (((0,), (0,)), ((), ())), preferred_element_type=F32)


def exchange_kernel(
    bos_h,
    grad_h,
    left_h,
    right_h,
    lgram_h,
    rgram_h,
    first_h,
    second_h,
    codes,
    scales,
    nlgram,
    nrgram,
    nfirst,
    nsecond,
    bos,
    grad,
    left,
    right,
    lgram,
    rgram,
    first,
    second,
    lt_hi,
    lt_lo,
    l_hi,
    l_lo,
    r_hi,
    r_lo,
    stage_in,
    land_in,
    owned,
    b_hi,
    b_lo,
    stage_out,
    stage_scale,
    load_sem,
    in_send,
    in_recv,
    out_send,
    out_recv,
    sc_sem,
):
    dp = lax.axis_index("dp")
    tp = lax.axis_index("tensor")
    me = dp * TP + tp

    loads = [
        pltpu.make_async_copy(src, dst, load_sem.at[i])
        for i, (src, dst) in enumerate(
            (
                (bos_h, bos),
                (grad_h, grad),
                (left_h, left),
                (right_h, right),
                (first_h, first),
                (second_h, second),
                (lgram_h, lgram),
                (rgram_h, rgram),
            )
        )
    ]
    for load in loads:
        load.start()

    barrier = pltpu.get_barrier_semaphore()

    def greet(d, t):
        pl.semaphore_signal(barrier, inc=1, device_id=(d, t), device_id_type=MESH)

    for i in range(1, TP):
        greet(dp, (tp + i) & (TP - 1))

    @pl.loop(1, DP)
    def _(j):
        for i in range(TP):
            greet((dp + j) & (DP - 1), (tp + i) & (TP - 1))

    loads[0].wait()
    loads[1].wait()
    for s in range(2):

        @pl.loop(0, DEV, step=8)
        def _(p):
            for i in range(8):
                stage_in[s, p + i] = grad[bos[2 * (p + i) + s]]

        land_in[s, me] = stage_in[s, me]

    pl.semaphore_wait(barrier, DEV - 1)

    def send_in(s, d, t):
        pltpu.make_async_remote_copy(
            stage_in.at[s, d * TP + t],
            land_in.at[s, me],
            in_send.at[s],
            in_recv.at[s],
            device_id=(d, t),
            device_id_type=MESH,
        ).start()

    for s in range(2):
        for i in range(1, TP):
            send_in(s, dp, (tp + i) & (TP - 1))

        @pl.loop(1, DP)
        def _(j):
            for i in range(TP):
                send_in(s, (dp + j) & (DP - 1), (tp + i) & (TP - 1))

    loads[2].wait()
    loads[3].wait()
    for s in range(2):

        @pl.loop(0, N, step=128)
        def _(r):
            rows = pl.ds(pl.multiple_of(r, 128), 128)
            hi, lo = split(left[s, rows, :])
            l_hi[s, rows, :] = hi
            l_lo[s, rows, :] = lo
            hi, lo = split(right[s, rows, :])
            r_hi[s, rows, :] = hi
            r_lo[s, rows, :] = lo
            hi, lo = split(left[s, :, rows].T)
            lt_hi[s, rows, :] = hi
            lt_lo[s, rows, :] = lo

    loads[4].wait()
    loads[5].wait()

    def all_of(ref, sem):
        pltpu.make_async_copy(ref, ref, sem).wait()

    for s in range(2):
        all_of(land_in.at[s, pl.ds(0, DEV - 1)], in_recv.at[s])
        for c in range(4):
            owned[s, :, c * 128 : (c + 1) * 128] = land_in[s, :, 4 * c : 4 * c + 4, :].reshape(N, 128)

        block = owned[s]
        a_hi, a_lo = split(dot(lt_hi[s], block) + dot(lt_lo[s], block))
        rotated = dot(a_hi, r_hi[s]) + (dot(a_hi, r_lo[s]) + dot(a_lo, r_hi[s]))
        nf = 0.9 * first[s] + 0.1 * rotated
        ns = 0.95 * second[s] + 0.05 * rotated * rotated
        nfirst[s] = nf
        nsecond[s] = ns
        n_hi, n_lo = split(nf / (jnp.sqrt(ns) + 1e-08))
        hi, lo = split(dot(l_hi[s], n_hi) + (dot(l_hi[s], n_lo) + dot(l_lo[s], n_hi)))
        b_hi[...] = hi.reshape(b_hi.shape)
        b_lo[...] = lo.reshape(b_lo.shape)

        for j in range(2):
            c = (dp + j) & 1
            hi = b_hi[:, c].reshape(N // 2, N)
            lo = b_lo[:, c].reshape(N // 2, N)
            result = dot_nt(hi, r_hi[s]) + (dot_nt(hi, r_lo[s]) + dot_nt(lo, r_hi[s]))
            top = jnp.maximum(jnp.max(jnp.abs(result), axis=1, keepdims=True), 1e-33)
            q = jnp.clip(jnp.round(result * (LEVELS / top)), -LEVELS, LEVELS).astype(jnp.int32)
            packed = (q[:, : N // 2] & 0xFFFF) | (q[:, N // 2 :] << 16)
            for h in range(2):
                stage_out[s, :, c, :, 4 * h : 4 * h + 4, :] = packed[:, h * 128 : (h + 1) * 128].reshape(
                    DP // 2, TP, 4, 128
                )
            step = jnp.broadcast_to(top * (1.0 / LEVELS), (N // 2, 128)).T
            for h in range(2):
                stage_scale[c, h, s] = step[:1, h * 128 : (h + 1) * 128]

            def send_out(g, t):
                pltpu.make_async_remote_copy(
                    stage_out.at[s, g, c, t],
                    codes.at[s, me],
                    out_send.at[s],
                    out_recv.at[s],
                    device_id=(2 * g + c, t),
                    device_id_type=MESH,
                ).start()
                if s == 1:
                    pltpu.make_async_remote_copy(
                        stage_scale.at[c, g // 4],
                        scales.at[me],
                        sc_sem.at[0],
                        sc_sem.at[1],
                        device_id=(2 * g + c, t),
                        device_id_type=MESH,
                    ).start()

            for i in range(1 if j == 0 else 0, TP):
                send_out(dp // 2, (tp + i) & (TP - 1))

            @pl.loop(1, DP // 2)
            def _(a):
                for i in range(TP):
                    send_out((dp // 2 + a) & (DP // 2 - 1), (tp + i) & (TP - 1))

        codes[s, me] = stage_out[s, dp // 2, dp & 1, tp]

    scales[me] = stage_scale[dp & 1, dp // 8]

    loads[6].wait()
    loads[7].wait()
    for s in range(2):
        nlgram[s] = 0.95 * lgram[s] + 0.05 * dot_nt(owned[s], owned[s])
        nrgram[s] = 0.95 * rgram[s] + 0.05 * dot_tn(owned[s], owned[s])

    for s in range(2):
        all_of(land_in.at[s, pl.ds(0, DEV - 1)], in_send.at[s])
        all_of(codes.at[s, pl.ds(0, DEV - 1)], out_send.at[s])
        all_of(codes.at[s, pl.ds(0, DEV - 1)], out_recv.at[s])
        all_of(scales.at[pl.ds(0, DEV - 1)], sc_sem.at[s])


def finish_kernel(bos_h, codes, scales, nlgram, nrgram, nfirst, nsecond, update, o_l, o_r, o_f, o_s, bos, upd, sem):
    dp = lax.axis_index("dp")
    tp = lax.axis_index("tensor")
    load = pltpu.make_async_copy(bos_h, bos, sem.at[5])
    load.start()
    moves = [
        pltpu.make_async_copy(src, dst, sem.at[i])
        for i, (src, dst) in enumerate(((nlgram, o_l), (nrgram, o_r), (nfirst, o_f), (nsecond, o_s)))
    ]
    for move in moves:
        move.start()
    lane = lax.broadcasted_iota(jnp.int32, (8, 128), 1)
    row = lax.broadcasted_iota(jnp.int32, (8, 128), 0)
    mine = lane == (((dp // 2) & 3) * TP + tp) * 4 + (row & 3)
    load.wait()

    for s in range(2):

        @pl.loop(0, DEV, step=32)
        def _(p):
            for i in range(32):
                b = bos[2 * (p + i) + s]
                v = codes[s, p + i]
                step = jnp.sum(
                    jnp.where(mine, jnp.broadcast_to(scales[p + i, s], (8, 128)), 0.0), axis=1, keepdims=True
                )
                upd[b, 0:8, :] = ((v << 16) >> 16).astype(F32) * step
                upd[b, 8:16, :] = (v >> 16).astype(F32) * step

    out = pltpu.make_async_copy(upd, update, sem.at[4])
    out.start()
    for move in moves:
        move.wait()
    out.wait()


def local(grad_blocks, block_of_slot, left_basis, right_basis, left_gram, right_gram, moment_first, moment_second):
    blocks = grad_blocks.shape[0]
    grad = grad_blocks.reshape(blocks, 4, 4, 128).transpose(0, 2, 1, 3).reshape(blocks, 16, 128)
    hbm = pl.BlockSpec(memory_space=pltpu.HBM)
    vmem = pl.BlockSpec(memory_space=pltpu.VMEM)
    square = (2, N, N)
    operands = [
        pltpu.with_memory_space_constraint(x, pltpu.HBM)
        for x in (
            block_of_slot,
            grad,
            left_basis,
            right_basis,
            left_gram,
            right_gram,
            moment_first,
            moment_second,
        )
    ]
    codes, scales, nlgram, nrgram, nfirst, nsecond = pl.pallas_call(
        exchange_kernel,
        out_shape=(
            pltpu.VMEM((2, DEV, 8, 128), jnp.int32),
            pltpu.VMEM((DEV, 2, 1, 128), F32),
            pltpu.VMEM(square, F32),
            pltpu.VMEM(square, F32),
            pltpu.VMEM(square, F32),
            pltpu.VMEM(square, F32),
        ),
        in_specs=[hbm] * 8,
        out_specs=(vmem,) * 6,
        scratch_shapes=[pltpu.SMEM((blocks,), jnp.int32), pltpu.VMEM((blocks, 16, 128), BF16)]
        + [pltpu.VMEM(square, F32)] * 6
        + [pltpu.VMEM(square, BF16)] * 6
        + [
            pltpu.VMEM((2, DEV, 16, 128), BF16),
            pltpu.VMEM((2, DEV, 16, 128), BF16),
            pltpu.VMEM(square, BF16),
            pltpu.VMEM((DP // 2, 2, 4 * TP, N), BF16),
            pltpu.VMEM((DP // 2, 2, 4 * TP, N), BF16),
            pltpu.VMEM((2, DP // 2, 2, TP, 8, 128), jnp.int32),
            pltpu.VMEM((2, 2, 2, 1, 128), F32),
            pltpu.SemaphoreType.DMA((8,)),
            pltpu.SemaphoreType.DMA((2,)),
            pltpu.SemaphoreType.DMA((2,)),
            pltpu.SemaphoreType.DMA((2,)),
            pltpu.SemaphoreType.DMA((2,)),
            pltpu.SemaphoreType.DMA((2,)),
        ],
        compiler_params=pltpu.CompilerParams(collective_id=0, has_side_effects=True, vmem_limit_bytes=44 << 20),
        name="exchange",
    )(*operands)
    update, *rest = pl.pallas_call(
        finish_kernel,
        out_shape=(jax.ShapeDtypeStruct((blocks, 16, 128), F32),) + (jax.ShapeDtypeStruct(square, F32),) * 4,
        in_specs=[hbm] + [vmem] * 6,
        out_specs=(hbm,) * 5,
        scratch_shapes=[
            pltpu.SMEM((blocks,), jnp.int32),
            pltpu.VMEM((blocks, 16, 128), F32),
            pltpu.SemaphoreType.DMA((6,)),
        ],
        compiler_params=pltpu.CompilerParams(vmem_limit_bytes=16 << 20),
        name="finish",
    )(operands[0], codes, scales, nlgram, nrgram, nfirst, nsecond)
    update = update.reshape(blocks, 4, 4, 128).transpose(0, 2, 1, 3).reshape(blocks, 4, N)
    return (update, *rest)


def solution(mesh):
    owner = P(("dp", "tensor"), None, None)
    rows = P(None, ("dp", "tensor"), None)
    return jax.shard_map(
        local,
        mesh=mesh,
        in_specs=(rows, P(), owner, owner, owner, owner, owner, owner),
        out_specs=(rows, owner, owner, owner, owner),
        check_vma=False,
    )
```

time: 56.5 us -> 46.3 us (0.82)
  Pallas kernels: 52.2 us -> 45.5 us
  local copies, waits for them, and re-layouts: 3.49 us -> 0 us
    pallas_call x1, Pallas kernels: 47.6 us -> 41.5 us  [local(): pl.pallas_call(exchange_kernel, out_shape=(pltpu.VMEM((2, DEV, 8, 128), j...]
    unnamed x6 -> x0, local copies, waits for them, and re-layouts: 3.49 us -> none
    pallas_call x1, Pallas kernels: 4.62 us -> 4.02 us  [local(): pl.pallas_call(finish_kernel, out_shape=(jax.ShapeDtypeStruct((blocks, 16...]
where the time goes in v2:
time: 46.3 us; the launch traced here: 46.1 us
  Pallas kernels  45.5 us (98%)
  between operations  0.64 us (1%)
    pallas_call x1, Pallas kernels, local(): pl.pallas_call(exchange_kernel, out_shape=(pltpu.VMEM((2, DEV, 8, 128), j...  41.5 us
    pallas_call x1, Pallas kernels, local(): pl.pallas_call(finish_kernel, out_shape=(jax.ShapeDtypeStruct((blocks, 16...  4.02 us

profile of v2, /device:TPU:1, one launch (start us, length us, event | category | flops | bytes accessed | tf_op | source)
XLA Modules:
  0.0 46.1 jit_solution(9912450406750010908)
XLA Ops:
  0.6 41.5 %exchange.1 = (s32[2,128,8,128]{3,2,1,0:T(8,128)S(1)}, f32[128,2,1,128]{3,2,1,0:T(1,128)S(1)}, f32[2,512,512]{2,1,0:T(8,128)S(1)}, f32[2,512,512]{2,1,0:T(8,128)...) custom-call(s32[256]{0:T(256)} %bos_h.3, bf16[256,16,128]{2,1,0:T(8,128)(2,1)} %bitcast.10, ...), custom_call_target="tpu_custom_call" | custom-call | tf_op jit(solution)/shard_map/exchange/pallas_call | solution.py:299
  42.1 4.0 %finish.1 = (f32[256,16,128]{2,1,0:T(8,128)}, f32[2,512,512]{2,1,0:T(8,128)}, f32[2,512,512]{2,1,0:T(8,128)}, f32[2,512,512]{2,1,0:T(8,128)}, f32[2,512,512]{2,1,0:T(8,128)}) custom-call(s32[256]{0:T(256)} %bos_h.3, s32[2,128,8,128]{3,2,1,0:T(8,128)S(1)} %get-tuple-element.16.codes, f32[128,2,1,128]{3,2,1,0:T(1,128)S(1)} %get-tuple-element.17.scales, ...), custom_call_target="tpu_custom_call" | custom-call | tf_op jit(solution)/shard_map/finish/pallas_call | solution.py:332

commit v3 on v2

v3 whole, which is shorter than its diff:
```python
import jax
import jax.numpy as jnp
from jax import lax
from jax.experimental import pallas as pl
from jax.experimental.pallas import tpu as pltpu
from jax.sharding import PartitionSpec as P

MESH = pl.DeviceIdType.MESH
F32 = jnp.float32
BF16 = jnp.bfloat16
N = 512
DP, TP = 16, 8
DEV = DP * TP
LEVELS = 32767.0


def split(x):
    hi = x.astype(BF16)
    return hi, (x - hi.astype(F32)).astype(BF16)


def dot(a, b):
    return jnp.dot(a, b, preferred_element_type=F32)


def dot_nt(a, b):
    return lax.dot_general(a, b, (((1,), (1,)), ((), ())), preferred_element_type=F32)


def dot_tn(a, b):
    return lax.dot_general(a, b, (((0,), (0,)), ((), ())), preferred_element_type=F32)


def scale_lanes(dp, tp, s):
    lane = lax.broadcasted_iota(jnp.int32, (8, 128), 1)
    row = lax.broadcasted_iota(jnp.int32, (8, 128), 0)
    return lane == 64 * s + (((dp // 2) & 1) * TP + tp) * 4 + (row & 3)


def decode(code, scale, mine):
    step = jnp.sum(jnp.where(mine, jnp.broadcast_to(scale, (8, 128)), 0.0), axis=1, keepdims=True)
    return ((code << 16) >> 16).astype(F32) * step, (code >> 16).astype(F32) * step


def exchange_kernel(
    bos_h,
    grad_h,
    left_h,
    right_h,
    lgram_h,
    rgram_h,
    first_h,
    second_h,
    codes,
    scales,
    rows_of_first,
    nlgram,
    nrgram,
    nfirst,
    nsecond,
    bos,
    grad,
    left,
    right,
    lgram,
    rgram,
    first,
    second,
    lt_hi,
    lt_lo,
    l_hi,
    l_lo,
    r_hi,
    r_lo,
    stage_in,
    land_in,
    owned,
    n_hi,
    n_lo,
    stage_out,
    stage_scale,
    step_of_first,
    load_sem,
    in_send,
    in_recv,
    out_send,
    out_recv,
    sc_sem,
):
    dp = lax.axis_index("dp")
    tp = lax.axis_index("tensor")
    me = dp * TP + tp

    loads = [
        pltpu.make_async_copy(src, dst, load_sem.at[i])
        for i, (src, dst) in enumerate(
            (
                (bos_h, bos),
                (grad_h, grad),
                (left_h, left),
                (right_h, right),
                (first_h, first),
                (second_h, second),
                (lgram_h, lgram),
                (rgram_h, rgram),
            )
        )
    ]
    for load in loads[:2]:
        load.start()

    barrier = pltpu.get_barrier_semaphore()

    def greet(d, t):
        pl.semaphore_signal(barrier, inc=1, device_id=(d, t), device_id_type=MESH)

    for i in range(1, TP):
        greet(dp, (tp + i) & (TP - 1))

    @pl.loop(1, DP)
    def _(j):
        for i in range(TP):
            greet((dp + j) & (DP - 1), (tp + i) & (TP - 1))

    for load in loads[2:]:
        load.start()

    loads[0].wait()
    loads[1].wait()
    for s in range(2):

        @pl.loop(0, DEV, step=8)
        def _(p):
            for i in range(8):
                stage_in[s, p + i] = grad[bos[2 * (p + i) + s]]

        land_in[s, dp // 2, dp & 1, tp] = stage_in[s, me]

    pl.semaphore_wait(barrier, DEV - 1)

    parts = ((2, 4, 6, 0), (8, 10, 12, 14), (1, 3, 5, 7), (9, 11, 13, 15))

    def send_in(s, part):
        def one(d, t):
            pltpu.make_async_remote_copy(
                stage_in.at[s, d * TP + t],
                land_in.at[s, dp // 2, dp & 1, tp],
                in_send.at[s, part],
                in_recv.at[s, part // 2],
                device_id=(d, t),
                device_id_type=MESH,
            ).start()

        for j in parts[part]:
            for i in range(TP):
                if i or j:
                    one((dp + j) & (DP - 1), (tp + i) & (TP - 1))

    def all_of(ref, sem):
        pltpu.make_async_copy(ref, ref, sem).wait()

    def sent_in(s, part):
        count = TP * len(parts[part]) - (0 in parts[part])
        all_of(stage_in.at[s, pl.ds(0, count)], in_send.at[s, part])

    for part in range(4):
        send_in(0, part)

    loads[2].wait()
    loads[3].wait()
    for s in range(2):

        @pl.loop(0, 4)
        def _(r):
            rows = pl.ds(pl.multiple_of(r * 128, 128), 128)
            hi, lo = split(right[s, rows, :])
            r_hi[s, rows, :] = hi
            r_lo[s, rows, :] = lo
            hi, lo = split(left[s, pl.ds(2 * r, 2)])
            l_hi[s, pl.ds(2 * r, 2)] = hi
            l_lo[s, pl.ds(2 * r, 2)] = lo
            for c in range(2):
                hi, lo = split(left[s, :, c, :, rows].reshape(N // 2, 128).T)
                lt_hi[s, c, rows, :] = hi
                lt_lo[s, c, rows, :] = lo

    loads[4].wait()
    loads[5].wait()

    for part in range(3):
        sent_in(0, part)
    send_in(1, 0)
    sent_in(0, 3)
    for part in range(1, 4):
        send_in(1, part)

    for s in range(2):
        half = []
        for j in range(2):
            c = (dp + j) & 1
            all_of(stage_in.at[s, pl.ds(0, DEV // 2 - 1 + j)], in_recv.at[s, j])
            for k in range(4):
                owned[s, :, c, :, k * 128 : (k + 1) * 128] = land_in[s, :, c, :, 4 * k : 4 * k + 4, :].reshape(
                    DP // 2, 4 * TP, 128
                )
            block = owned[s, :, c].reshape(N // 2, N)
            half.append(dot(lt_hi[s, c], block) + dot(lt_lo[s, c], block))
        a_hi, a_lo = split(half[0] + half[1])
        rotated = dot(a_hi, r_hi[s]) + (dot(a_hi, r_lo[s]) + dot(a_lo, r_hi[s]))
        nf = 0.9 * first[s] + 0.1 * rotated
        ns = 0.95 * second[s] + 0.05 * rotated * rotated
        nfirst[s] = nf
        nsecond[s] = ns
        hi, lo = split(nf / (jnp.sqrt(ns) + 1e-08))
        n_hi[...] = hi
        n_lo[...] = lo

        for j in range(2):
            c = (dp + j) & 1
            left_hi = l_hi[s, :, c].reshape(N // 2, N)
            left_lo = l_lo[s, :, c].reshape(N // 2, N)
            hi, lo = split(dot(left_hi, n_hi[...]) + (dot(left_hi, n_lo[...]) + dot(left_lo, n_hi[...])))
            result = dot_nt(hi, r_hi[s]) + (dot_nt(hi, r_lo[s]) + dot_nt(lo, r_hi[s]))
            top = jnp.maximum(jnp.max(jnp.abs(result), axis=1, keepdims=True), 1e-33)
            q = jnp.clip(jnp.round(result * (LEVELS / top)), -LEVELS, LEVELS).astype(jnp.int32)
            packed = (q[:, : N // 2] & 0xFFFF) | (q[:, N // 2 :] << 16)
            for h in range(2):
                stage_out[s, :, c, :, 4 * h : 4 * h + 4, :] = packed[:, h * 128 : (h + 1) * 128].reshape(
                    DP // 2, TP, 4, 128
                )
            step = jnp.broadcast_to(top * (1.0 / LEVELS), (N // 2, 128)).T
            if s == 0:
                step_of_first[c] = step[:1, :]
            else:
                for h in range(4):
                    part = slice(64 * h, 64 * h + 64)
                    stage_scale[c, h] = jnp.concatenate([step_of_first[c][:, part], step[:1, part]], axis=1)

            def send_out(g, t):
                pltpu.make_async_remote_copy(
                    stage_out.at[s, g, c, t],
                    codes.at[s, me],
                    out_send.at[s],
                    out_recv.at[s],
                    device_id=(2 * g + c, t),
                    device_id_type=MESH,
                ).start()

            def send_scale(g, t):
                pltpu.make_async_remote_copy(
                    stage_scale.at[c, g // 2],
                    scales.at[me],
                    sc_sem.at[0],
                    sc_sem.at[1],
                    device_id=(2 * g + c, t),
                    device_id_type=MESH,
                ).start()

            def to_all(send):
                for i in range(1 if j == 0 else 0, TP):
                    send(dp // 2, (tp + i) & (TP - 1))

                @pl.loop(1, DP // 2)
                def _(a):
                    for i in range(TP):
                        send((dp // 2 + a) & (DP // 2 - 1), (tp + i) & (TP - 1))

            if s == 1:
                to_all(send_scale)
            to_all(send_out)

        codes[s, me] = stage_out[s, dp // 2, dp & 1, tp]

    scales[me] = stage_scale[dp & 1, dp // 4]

    loads[6].wait()
    loads[7].wait()
    for s in range(2):
        block = owned[s].reshape(N, N)
        nlgram[s] = 0.95 * lgram[s] + 0.05 * dot_nt(block, block)
        nrgram[s] = 0.95 * rgram[s] + 0.05 * dot_tn(block, block)
    all_of(scales.at[pl.ds(0, DEV - 1)], sc_sem.at[1])
    all_of(codes.at[0, pl.ds(0, DEV - 1)], out_recv.at[0])
    mine = scale_lanes(dp, tp, 0)

    @pl.loop(0, DEV, step=32)
    def _(p):
        for i in range(32):
            low, high = decode(codes[0, p + i], scales[p + i], mine)
            rows_of_first[p + i, 0:8, :] = low
            rows_of_first[p + i, 8:16, :] = high

    for part in range(4):
        sent_in(1, part)
    all_of(scales.at[pl.ds(0, DEV - 1)], sc_sem.at[0])
    for s in range(2):
        all_of(codes.at[s, pl.ds(0, DEV - 1)], out_send.at[s])
    all_of(codes.at[1, pl.ds(0, DEV - 1)], out_recv.at[1])


def finish_kernel(
    bos_h, codes, scales, rows_of_first, nlgram, nrgram, nfirst, nsecond, update, o_l, o_r, o_f, o_s, bos, rows, sem
):
    dp = lax.axis_index("dp")
    tp = lax.axis_index("tensor")
    load = pltpu.make_async_copy(bos_h, bos, sem.at[5])
    load.start()
    moves = [
        pltpu.make_async_copy(src, dst, sem.at[i])
        for i, (src, dst) in enumerate(((nlgram, o_l), (nrgram, o_r), (nfirst, o_f), (nsecond, o_s)))
    ]
    for move in moves:
        move.start()
    mine = scale_lanes(dp, tp, 1)
    load.wait()

    @pl.loop(0, DEV, step=32)
    def _(p):
        for i in range(32):
            pltpu.make_async_copy(rows_of_first.at[p + i], update.at[bos[2 * (p + i)]], sem.at[4]).start()

    @pl.loop(0, DEV, step=32)
    def _(p):
        for i in range(32):
            low, high = decode(codes[1, p + i], scales[p + i], mine)
            rows[p + i, 0:8, :] = low
            rows[p + i, 8:16, :] = high
        for i in range(32):
            pltpu.make_async_copy(rows.at[p + i], update.at[bos[2 * (p + i) + 1]], sem.at[4]).start()

    for move in moves:
        move.wait()
    pltpu.make_async_copy(update, update, sem.at[4]).wait()


def local(grad_blocks, block_of_slot, left_basis, right_basis, left_gram, right_gram, moment_first, moment_second):
    blocks = grad_blocks.shape[0]
    grad = grad_blocks.reshape(blocks, 4, 4, 128).transpose(0, 2, 1, 3).reshape(blocks, 16, 128)
    hbm = pl.BlockSpec(memory_space=pltpu.HBM)
    vmem = pl.BlockSpec(memory_space=pltpu.VMEM)
    square = (2, N, N)
    by_core = (2, DP // 2, 2, 4 * TP, N)
    operands = [
        pltpu.with_memory_space_constraint(x, pltpu.HBM)
        for x in (
            block_of_slot,
            grad,
            left_basis.reshape(by_core),
            right_basis,
            left_gram,
            right_gram,
            moment_first,
            moment_second,
        )
    ]
    codes, scales, rows_of_first, nlgram, nrgram, nfirst, nsecond = pl.pallas_call(
        exchange_kernel,
        out_shape=(
            pltpu.VMEM((2, DEV, 8, 128), jnp.int32),
            pltpu.VMEM((DEV, 1, 128), F32),
            pltpu.VMEM((DEV, 16, 128), F32),
            pltpu.VMEM(square, F32),
            pltpu.VMEM(square, F32),
            pltpu.VMEM(square, F32),
            pltpu.VMEM(square, F32),
        ),
        in_specs=[hbm] * 8,
        out_specs=(vmem,) * 7,
        scratch_shapes=[pltpu.SMEM((blocks,), jnp.int32), pltpu.VMEM((blocks, 16, 128), BF16)]
        + [pltpu.VMEM(by_core, F32)]
        + [pltpu.VMEM(square, F32)] * 5
        + [pltpu.VMEM((2, 2, N, N // 2), BF16)] * 2
        + [pltpu.VMEM(by_core, BF16)] * 2
        + [pltpu.VMEM(square, BF16)] * 2
        + [
            pltpu.VMEM((2, DEV, 16, 128), BF16),
            pltpu.VMEM((2, DP // 2, 2, TP, 16, 128), BF16),
            pltpu.VMEM(by_core, BF16),
            pltpu.VMEM((N, N), BF16),
            pltpu.VMEM((N, N), BF16),
            pltpu.VMEM((2, DP // 2, 2, TP, 8, 128), jnp.int32),
            pltpu.VMEM((2, 4, 1, 128), F32),
            pltpu.VMEM((2, 1, N // 2), F32),
            pltpu.SemaphoreType.DMA((8,)),
            pltpu.SemaphoreType.DMA((2, 4)),
            pltpu.SemaphoreType.DMA((2, 2)),
            pltpu.SemaphoreType.DMA((2,)),
            pltpu.SemaphoreType.DMA((2,)),
            pltpu.SemaphoreType.DMA((2,)),
        ],
        compiler_params=pltpu.CompilerParams(collective_id=0, has_side_effects=True, vmem_limit_bytes=44 << 20),
        name="exchange",
    )(*operands)
    update, *rest = pl.pallas_call(
        finish_kernel,
        out_shape=(jax.ShapeDtypeStruct((blocks, 16, 128), F32),) + (jax.ShapeDtypeStruct(square, F32),) * 4,
        in_specs=[hbm] + [vmem] * 7,
        out_specs=(hbm,) * 5,
        scratch_shapes=[
            pltpu.SMEM((blocks,), jnp.int32),
            pltpu.VMEM((DEV, 16, 128), F32),
            pltpu.SemaphoreType.DMA((6,)),
        ],
        compiler_params=pltpu.CompilerParams(vmem_limit_bytes=16 << 20),
        name="finish",
    )(operands[0], codes, scales, rows_of_first, nlgram, nrgram, nfirst, nsecond)
    update = update.reshape(blocks, 4, 4, 128).transpose(0, 2, 1, 3).reshape(blocks, 4, N)
    return (update, *rest)


def solution(mesh):
    owner = P(("dp", "tensor"), None, None)
    rows = P(None, ("dp", "tensor"), None)
    return jax.shard_map(
        local,
        mesh=mesh,
        in_specs=(rows, P(), owner, owner, owner, owner, owner, owner),
        out_specs=(rows, owner, owner, owner, owner),
        check_vma=False,
    )
```

time: 46.3 us -> 44.5 us (0.961)
  Pallas kernels: 45.5 us -> 43.7 us
    pallas_call x1, Pallas kernels: 41.5 us -> 39.5 us  [local(): pl.pallas_call(exchange_kernel, out_shape=(pltpu.VMEM((2, DEV, 8, 128), j...]
where the time goes in v3:
time: 44.5 us; the launch traced here: 44.4 us
  Pallas kernels  43.7 us (98%)
  between operations  0.64 us (1%)
    pallas_call x1, Pallas kernels, local(): pl.pallas_call(exchange_kernel, out_shape=(pltpu.VMEM((2, DEV, 8, 128), j...  39.5 us
    pallas_call x1, Pallas kernels, local(): pl.pallas_call(finish_kernel, out_shape=(jax.ShapeDtypeStruct((blocks, 16...  4.24 us

profile of v3, /device:TPU:1, one launch (start us, length us, event | category | flops | bytes accessed | tf_op | source)
XLA Modules:
  0.0 44.4 jit_solution(10850918317801512425)
XLA Ops:
  0.6 39.5 %exchange.1 = (s32[2,128,8,128]{3,2,1,0:T(8,128)S(1)}, f32[128,1,128]{2,1,0:T(1,128)S(1)}, f32[128,16,128]{2,1,0:T(8,128)S(1)}, f32[2,512,512]{2,1,0:T(8,128)S(1...) custom-call(s32[256]{0:T(256)} %bos_h.3, bf16[256,16,128]{2,1,0:T(8,128)(2,1)} %bitcast.12, ...), custom_call_target="tpu_custom_call" | custom-call | tf_op jit(solution)/shard_map/exchange/pallas_call | solution.py:356
  40.1 4.2 %finish.1 = (f32[256,16,128]{2,1,0:T(8,128)}, f32[2,512,512]{2,1,0:T(8,128)}, f32[2,512,512]{2,1,0:T(8,128)}, f32[2,512,512]{2,1,0:T(8,128)}, f32[2,512,512]{2,1,0:T(8,128)}) custom-call(s32[256]{0:T(256)} %bos_h.3, s32[2,128,8,128]{3,2,1,0:T(8,128)S(1)} %get-tuple-element.17.codes, f32[128,1,128]{2,1,0:T(1,128)S(1)} %get-tuple-element.18.scales, ...), custom_call_target="tpu_custom_call" | custom-call | tf_op jit(solution)/shard_map/finish/pallas_call | solution.py:394

commit v4 on v3

--- a/solution.py
+++ b/solution.py
@@ -127,8 +127,7 @@
 
     loads[0].wait()
     loads[1].wait()
-    for s in range(2):
-
+    def gather(s):
         @pl.loop(0, DEV, step=8)
         def _(p):
             for i in range(8):
@@ -136,9 +135,8 @@
 
         land_in[s, dp // 2, dp & 1, tp] = stage_in[s, me]
 
+    gather(0)
     pl.semaphore_wait(barrier, DEV - 1)
-
-    parts = ((2, 4, 6, 0), (8, 10, 12, 14), (1, 3, 5, 7), (9, 11, 13, 15))
 
     def send_in(s, part):
         def one(d, t):
@@ -151,20 +149,25 @@
                 device_id_type=MESH,
             ).start()
 
-        for j in parts[part]:
+        if part == 0:
+            for i in range(1, TP):
+                one(dp, (tp + i) & (TP - 1))
+
+        @pl.loop(1 if part == 0 else 0, 4)
+        def _(k):
+            j = 8 * (part % 2) + 2 * k + part // 2
             for i in range(TP):
-                if i or j:
-                    one((dp + j) & (DP - 1), (tp + i) & (TP - 1))
+                one((dp + j) & (DP - 1), (tp + i) & (TP - 1))
 
     def all_of(ref, sem):
         pltpu.make_async_copy(ref, ref, sem).wait()
 
     def sent_in(s, part):
-        count = TP * len(parts[part]) - (0 in parts[part])
-        all_of(stage_in.at[s, pl.ds(0, count)], in_send.at[s, part])
+        all_of(stage_in.at[s, pl.ds(0, DEV // 4 - (part == 0))], in_send.at[s, part])
 
     for part in range(4):
         send_in(0, part)
+    gather(1)
 
     loads[2].wait()
     loads[3].wait()
@@ -204,9 +207,11 @@
                     DP // 2, 4 * TP, 128
                 )
             block = owned[s, :, c].reshape(N // 2, N)
-            half.append(dot(lt_hi[s, c], block) + dot(lt_lo[s, c], block))
-        a_hi, a_lo = split(half[0] + half[1])
-        rotated = dot(a_hi, r_hi[s]) + (dot(a_hi, r_lo[s]) + dot(a_lo, r_hi[s]))
+            part_hi, part_lo = split(dot(block, r_hi[s]) + dot(block, r_lo[s]))
+            half.append(
+                dot(lt_hi[s, c], part_hi) + (dot(lt_hi[s, c], part_lo) + dot(lt_lo[s, c], part_hi))
+            )
+        rotated = half[0] + half[1]
         nf = 0.9 * first[s] + 0.1 * rotated
         ns = 0.95 * second[s] + 0.05 * rotated * rotated
         nfirst[s] = nf
@@ -265,9 +270,11 @@
                     for i in range(TP):
                         send((dp // 2 + a) & (DP // 2 - 1), (tp + i) & (TP - 1))
 
-            if s == 1:
+            if s == 1 and j == 1:
                 to_all(send_scale)
             to_all(send_out)
+            if s == 1 and j == 0:
+                to_all(send_scale)
 
         codes[s, me] = stage_out[s, dp // 2, dp & 1, tp]
 
@@ -283,9 +290,9 @@
     all_of(codes.at[0, pl.ds(0, DEV - 1)], out_recv.at[0])
     mine = scale_lanes(dp, tp, 0)
 
-    @pl.loop(0, DEV, step=32)
+    @pl.loop(0, DEV, step=16)
     def _(p):
-        for i in range(32):
+        for i in range(16):
             low, high = decode(codes[0, p + i], scales[p + i], mine)
             rows_of_first[p + i, 0:8, :] = low
             rows_of_first[p + i, 8:16, :] = high
@@ -317,20 +324,21 @@
     @pl.loop(0, DEV, step=32)
     def _(p):
         for i in range(32):
-            pltpu.make_async_copy(rows_of_first.at[p + i], update.at[bos[2 * (p + i)]], sem.at[4]).start()
+            rows[bos[2 * (p + i)]] = rows_of_first[p + i]
 
     @pl.loop(0, DEV, step=32)
     def _(p):
         for i in range(32):
             low, high = decode(codes[1, p + i], scales[p + i], mine)
-            rows[p + i, 0:8, :] = low
-            rows[p + i, 8:16, :] = high
-        for i in range(32):
-            pltpu.make_async_copy(rows.at[p + i], update.at[bos[2 * (p + i) + 1]], sem.at[4]).start()
-
+            b = bos[2 * (p + i) + 1]
+            rows[b, 0:8, :] = low
+            rows[b, 8:16, :] = high
+
+    out = pltpu.make_async_copy(rows, update, sem.at[4])
+    out.start()
     for move in moves:
         move.wait()
-    pltpu.make_async_copy(update, update, sem.at[4]).wait()
+    out.wait()
 
 
 def local(grad_blocks, block_of_slot, left_basis, right_basis, left_gram, right_gram, moment_first, moment_second):
@@ -398,7 +406,7 @@
         out_specs=(hbm,) * 5,
         scratch_shapes=[
             pltpu.SMEM((blocks,), jnp.int32),
-            pltpu.VMEM((DEV, 16, 128), F32),
+            pltpu.VMEM((blocks, 16, 128), F32),
             pltpu.SemaphoreType.DMA((6,)),
         ],
         compiler_params=pltpu.CompilerParams(vmem_limit_bytes=16 << 20),

time: 44.5 us -> 43.7 us (0.982)
  Pallas kernels: 43.7 us -> 42.9 us
    pallas_call x1, Pallas kernels: 39.5 us -> 38.9 us  [local(): pl.pallas_call(exchange_kernel, out_shape=(pltpu.VMEM((2, DEV, 8, 128), j...]
where the time goes in v4:
time: 43.7 us; the launch traced here: 43.5 us
  Pallas kernels  42.9 us (98%)
  between operations  0.64 us (1%)
    pallas_call x1, Pallas kernels, local(): pl.pallas_call(exchange_kernel, out_shape=(pltpu.VMEM((2, DEV, 8, 128), j...  38.9 us
    pallas_call x1, Pallas kernels, local(): pl.pallas_call(finish_kernel, out_shape=(jax.ShapeDtypeStruct((blocks, 16...  4.02 us

profile of v4, /device:TPU:1, one launch (start us, length us, event | category | flops | bytes accessed | tf_op | source)
XLA Modules:
  0.0 43.5 jit_solution(9898095987247729455)
XLA Ops:
  0.6 38.9 %exchange.1 = (s32[2,128,8,128]{3,2,1,0:T(8,128)S(1)}, f32[128,1,128]{2,1,0:T(1,128)S(1)}, f32[128,16,128]{2,1,0:T(8,128)S(1)}, f32[2,512,512]{2,1,0:T(8,128)S(1...) custom-call(s32[256]{0:T(256)} %bos_h.3, bf16[256,16,128]{2,1,0:T(8,128)(2,1)} %bitcast.12, ...), custom_call_target="tpu_custom_call" | custom-call | tf_op jit(solution)/shard_map/exchange/pallas_call | solution.py:364
  39.5 4.0 %finish.1 = (f32[256,16,128]{2,1,0:T(8,128)}, f32[2,512,512]{2,1,0:T(8,128)}, f32[2,512,512]{2,1,0:T(8,128)}, f32[2,512,512]{2,1,0:T(8,128)}, f32[2,512,512]{2,1,0:T(8,128)}) custom-call(s32[256]{0:T(256)} %bos_h.3, s32[2,128,8,128]{3,2,1,0:T(8,128)S(1)} %get-tuple-element.17.codes, f32[128,1,128]{2,1,0:T(1,128)S(1)} %get-tuple-element.18.scales, ...), custom_call_target="tpu_custom_call" | custom-call | tf_op jit(solution)/shard_map/finish/pallas_call | solution.py:402

commit v5 on v4

--- a/solution.py
+++ b/solution.py
@@ -189,13 +189,20 @@
 
     loads[4].wait()
     loads[5].wait()
-
     for part in range(3):
         sent_in(0, part)
     send_in(1, 0)
     sent_in(0, 3)
     for part in range(1, 4):
         send_in(1, part)
+
+    for s in range(2):
+
+        @pl.loop(0, 4)
+        def _(r):
+            rows = pl.ds(pl.multiple_of(r * 128, 128), 128)
+            first[s, rows, :] = 0.9 * first[s, rows, :]
+            second[s, rows, :] = 0.95 * second[s, rows, :]
 
     for s in range(2):
         half = []
@@ -212,8 +219,8 @@
                 dot(lt_hi[s, c], part_hi) + (dot(lt_hi[s, c], part_lo) + dot(lt_lo[s, c], part_hi))
             )
         rotated = half[0] + half[1]
-        nf = 0.9 * first[s] + 0.1 * rotated
-        ns = 0.95 * second[s] + 0.05 * rotated * rotated
+        nf = first[s] + 0.1 * rotated
+        ns = second[s] + 0.05 * rotated * rotated
         nfirst[s] = nf
         nsecond[s] = ns
         hi, lo = split(nf / (jnp.sqrt(ns) + 1e-08))

time: 43.7 us -> 43.6 us (level)
  no operation moved by 1% of the time
where the time goes in v5:
time: 43.6 us; the launch traced here: 43.5 us
  Pallas kernels  42.8 us (98%)
  between operations  0.64 us (1%)
    pallas_call x1, Pallas kernels, local(): pl.pallas_call(exchange_kernel, out_shape=(pltpu.VMEM((2, DEV, 8, 128), j...  38.8 us
    pallas_call x1, Pallas kernels, local(): pl.pallas_call(finish_kernel, out_shape=(jax.ShapeDtypeStruct((blocks, 16...  4.02 us

profile of v5, /device:TPU:1, one launch (start us, length us, event | category | flops | bytes accessed | tf_op | source)
XLA Modules:
  0.0 43.5 jit_solution(5785980532676348744)
XLA Ops:
  0.6 38.8 %exchange.1 = (s32[2,128,8,128]{3,2,1,0:T(8,128)S(1)}, f32[128,1,128]{2,1,0:T(1,128)S(1)}, f32[128,16,128]{2,1,0:T(8,128)S(1)}, f32[2,512,512]{2,1,0:T(8,128)S(1...) custom-call(s32[256]{0:T(256)} %bos_h.3, bf16[256,16,128]{2,1,0:T(8,128)(2,1)} %bitcast.12, ...), custom_call_target="tpu_custom_call" | custom-call | tf_op jit(solution)/shard_map/exchange/pallas_call | solution.py:371
  39.5 4.0 %finish.1 = (f32[256,16,128]{2,1,0:T(8,128)}, f32[2,512,512]{2,1,0:T(8,128)}, f32[2,512,512]{2,1,0:T(8,128)}, f32[2,512,512]{2,1,0:T(8,128)}, f32[2,512,512]{2,1,0:T(8,128)}) custom-call(s32[256]{0:T(256)} %bos_h.3, s32[2,128,8,128]{3,2,1,0:T(8,128)S(1)} %get-tuple-element.17.codes, f32[128,1,128]{2,1,0:T(1,128)S(1)} %get-tuple-element.18.scales, ...), custom_call_target="tpu_custom_call" | custom-call | tf_op jit(solution)/shard_map/finish/pallas_call | solution.py:409
